TPU v7x, 128 devices: a whole 4x4x4 slice. The times are simulated.
128 devices in a mesh: wide: 16 (over y, x_hi, core), band: 8 (over z, x_lo).
Axes of the slice: x: 4 (x_hi: 2, x_lo: 2; x = x_hi * 2 + x_lo), y: 4, z: 4, core: 2. Of those that a mesh axis runs over, the one named last changes fastest.
Arguments:
- samples: bfloat16 [16, 512, 18432], P(None, 'band', 'wide'), may hold values from -12 to 12
- offsets: int32 [32], P('wide'), may hold values from 0 to 64
Outputs:
- correlations: bfloat16 [2, 512, 8192, 128], P(None, 'band', 'wide')
All inputs are finite; a program needn't handle non-finite values.
Results may differ from a plain program's by a relative error of at most 0.0065.
Values may be sent and summed in bfloat16 or wider, within the bound.
A program may use at most 192 MiB of HBM per device.

v0:
```python
import math

import jax
import jax.numpy as jnp
import ml_dtypes
import numpy as np
from jax import lax
from jax.experimental import pallas as pl
from jax.experimental.pallas import tpu as pltpu
from jax.sharding import PartitionSpec as P

MESH = pl.DeviceIdType.MESH
NQ = 4
NJ = 8
PW = 24
NA = 7
PITCH = 264
FAC = 1 / math.sqrt(32)


def dft_np():
    n=np.arange(512); f=np.arange(256)
    ph=(f[:,None]*n[None,:])%512
    ang=2*np.pi/512*ph
    win=0.5-0.5*np.cos(2*np.pi/512*(n+0.5))
    t=np.concatenate([np.cos(ang)*win, -np.sin(ang)*win],0).astype(ml_dtypes.bfloat16)
    t=t.reshape(2,32,8,512).transpose(1,0,2,3).reshape(512,512).astype(np.float32)
    return np.concatenate([t,np.zeros((512,128),np.float32)],1)

def lag_np():
    f=np.arange(256); l=np.arange(128)-64
    ph=(f[:,None]*l[None,:])%512
    ang=2*np.pi/512*ph
    t=np.concatenate([np.cos(ang)/16,-np.sin(ang)/16],0).astype(ml_dtypes.bfloat16)
    return t.T.copy()

def spec_kernel(off_ref, tab_ref, s_ref, x_ref, tk):
    i=pl.program_id(0)
    @pl.when(i==0)
    def _():
        for k in range(2):
            t=pltpu.roll(tab_ref[...], off_ref[k]+64*k, 1)
            tk[k]=t.astype(jnp.bfloat16)
    s=s_ref[...].reshape(128,1152)
    a0=lax.dot_general(tk[0], s[:, :640], (((1,),(1,)),((),())), preferred_element_type=jnp.float32)
    a1=lax.dot_general(tk[1], s[:, 512:], (((1,),(1,)),((),())), preferred_element_type=jnp.float32)
    lane=lax.broadcasted_iota(jnp.int32,(512,128),1)<64
    g0=jnp.where(lane,a0,pltpu.roll(a1,64,1))
    g1=jnp.where(lane,pltpu.roll(a0,64,1),a1)
    for j,g in enumerate((g0,g1)):
        v=g.reshape(32,2,8,128)
        re=v[:,0]; im=v[:,1]
        pw=re*re+im*im
        level=jnp.sum(jnp.sum(pw,0),0,keepdims=True)*(0.25/256.0)+1e-6
        inv=lax.rsqrt(pw+level[None])
        x_ref[j]=jnp.stack([re*inv,im*inv],1).reshape(32,16,128).astype(jnp.bfloat16)

def spectra(samples, offsets):
    return pl.pallas_call(spec_kernel,
      grid=(8,),
      in_specs=[pl.BlockSpec(memory_space=pltpu.SMEM), pl.BlockSpec((512,640),lambda i:(0,0)), pl.BlockSpec((2,64,1152),lambda i:(i,0,0))],
      out_specs=pl.BlockSpec((2,32,16,128),lambda i:(i,0,0,0)),
      out_shape=jax.ShapeDtypeStruct((16,32,16,128),jnp.bfloat16),
      scratch_shapes=[pltpu.VMEM((2,512,640),jnp.bfloat16)],
      compiler_params=pltpu.CompilerParams(vmem_limit_bytes=32*2**20),
    )(offsets, jnp.asarray(dft_np()), samples)

def relayout_quarter(rcv, tmp, hold, q):
    @pl.loop(0, 8)
    def _(fi):
        fg=q*8+fi
        for xs in range(2):
            for w in range(8):
                tmp[xs, w*PW:w*PW+16, :]=rcv[xs, w, fg].astype(jnp.float32)
        for xs in range(2):
            for f8 in range(8):
                re=tmp[xs, pl.ds(f8,8,stride=PW),:]
                im=tmp[xs, pl.ds(8+f8,8,stride=PW),:]
                hold[xs, fg*8+f8]=jnp.concatenate([re,im],0).astype(jnp.bfloat16)

def join2(a,b):
    return jnp.concatenate([a[:,:64],b[:,:64]],1), jnp.concatenate([a[:,64:],b[:,64:]],1)


def prep_rows(r_ref,fg,tmp,rt):
    for w in range(16):
        y,xs,c=w//4,(w//2)%2,w%2
        for g in range(2):
            tmp[g,xs,(y*2+c)*PW:(y*2+c)*PW+16,:]=r_ref[w,g,fg].astype(jnp.float32)
    for fp in range(4):
        ks=[];ts=[]
        for f8 in (2*fp,2*fp+1):
            parts=[]
            for g in range(2):
                re=[tmp[g,xs,pl.ds(f8,8,stride=PW),:] for xs in range(2)]
                im=[tmp[g,xs,pl.ds(8+f8,8,stride=PW),:] for xs in range(2)]
                parts.append((jnp.concatenate([re[0],im[0],re[1],im[1]],0), jnp.concatenate([im[0],-re[0],im[1],-re[1]],0)))
            ks+=join2(parts[0][0],parts[1][0])
            ts+=join2(parts[0][1],parts[1][1])
        rt[fg*4+fp,0:128]=jnp.concatenate(ks,0).T.astype(jnp.bfloat16)
        rt[fg*4+fp,128:256]=jnp.concatenate(ts,0).T.astype(jnp.bfloat16)


def stage_one(gs,rt,scr,f0,pairs):
    zero=jnp.zeros((64,128),jnp.bfloat16)
    for i in range(pairs):
        parts=[]
        for j in range(2):
            f=f0+2*i+j
            c=jnp.concatenate(join2(gs[0,:,f].reshape(32,128),gs[1,:,f].reshape(32,128)),0)
            parts.append(jnp.concatenate([c,zero] if j==0 else [zero,c],1))
        s=jnp.dot(rt[f0//2+i],jnp.concatenate(parts,0),preferred_element_type=jnp.float32)
        for j in range(2):
            scr[pl.ds(pl.multiple_of((f0+2*i+j)*PITCH,8),256),:]=s[:,j*128:(j+1)*128]


def stage_two(scr,lag,ost,slot_,r0,pairs,row_base,col_base):
    for i in range(pairs):
        rows=[r0+2*i+j for j in range(2)]
        rhs=jnp.concatenate([jnp.concatenate([scr[pl.ds(p*128+r,256,stride=PITCH),:].astype(jnp.bfloat16) for p in range(2)],0) for r in rows],1)
        o=jnp.dot(lag,rhs,preferred_element_type=jnp.float32)
        for j in range(2):
            r=r0+2*i+j
            oc=(o[:,j*128:(j+1)*128]*FAC).T
            row=(r//64)*512+row_base+r%64
            col=col_base+lax.broadcasted_iota(jnp.int32,(128,128),0)
            ost[slot_,2*i+j]=jnp.where(col==row,0.0,oc).astype(jnp.bfloat16)


def main_kernel(x_ref, lag_ref, out_ref, g2_ref, rt_out, r_ref, rcv, tmp, hold, rtmp, rt, gs, scr, ost,
                a_send, a_recv, r_send, r_recv, x_send, zp_send, zm_send, g_recv, l_sem, g_sem, o_sem, t_sem):
    wide=lax.axis_index("wide"); band=lax.axis_index("band")
    y=wide//4; xhi=(wide//2)%2; core=wide%2
    z=band//2; xl=band%2
    zp=(z+1)%4; zm=(z+3)%4; z2=(z+2)%4
    def wid(y_,xh_,c_): return (y_*2+xh_)*2+c_
    def a2a_dev(t):
        dy=t//4; dx=(t//2)%2; dc=t%2
        y_=(y+dy)%4; xh_=(xhi+dx)%2; c_=(core+dc)%2
        return y_,xh_,c_,dx
    dev_x=(wide, z*2+(1-xl)); dev_zp=(wide, zp*2+xl); dev_zm=(wide, zm*2+xl)
    dev_xhi=(wid(y,1-xhi,core), band)
    dev_core=(wid(y,xhi,1-core), band)
    bar=pltpu.get_barrier_semaphore()
    @pl.loop(1,16)
    def _(t):
        y_,xh_,c_,dx=a2a_dev(t)
        pl.semaphore_signal(bar,1,device_id=(wid(y_,xh_,c_), z*2+(xl+dx)%2),device_id_type=MESH)
    for d in (dev_x,dev_zp,dev_zm,dev_xhi):
        pl.semaphore_signal(bar,1,device_id=d,device_id_type=MESH)
    pl.semaphore_wait(bar,19)

    def rc(src,dst,ss,rs,dev):
        return pltpu.make_async_remote_copy(src_ref=src,dst_ref=dst,send_sem=ss,recv_sem=rs,device_id=dev,device_id_type=MESH)

    row_src=x_ref.at[pl.ds(0,2)]
    rows_xhi=rc(row_src, r_ref.at[wide], r_send.at[0], r_recv.at[wide], dev_xhi)
    row_local=pltpu.make_async_copy(row_src, r_ref.at[wide], l_sem.at[0])
    row_local.start()
    own_local=pltpu.make_async_copy(x_ref.at[wide], rcv.at[xhi, y*2+core], l_sem.at[1])
    own_local.start()
    def a2a_copy(t,q):
        y_,xh_,c_,dx=a2a_dev(t)
        fs=pl.ds(q*8,8)
        return rc(x_ref.at[wid(y_,xh_,c_),fs], rcv.at[xhi,y*2+core,fs], a_send.at[t,q], a_recv.at[wide,q],
                  (wid(y_,xh_,c_), z*2+(xl+dx)%2))
    def a2a_wait(t,q):
        dy=t//4; dx=(t//2)%2; dc=t%2
        y_=(y+4-dy)%4; xh_=(xhi+dx)%2; c_=(core+dc)%2
        fs=pl.ds(q*8,8)
        s=wid(y_,xh_,c_)
        rc(x_ref.at[s,fs], rcv.at[xh_,y_*2+c_,fs], a_send.at[t,q], a_recv.at[s,q], dev_x).wait_recv()
    for q in range(2):
        @pl.loop(1,16)
        def _(t):
            a2a_copy(t,q).start()
    def row_y(dy,s,slot):
        return rc(r_ref.at[s], r_ref.at[s], r_send.at[slot], r_recv.at[s], (wid((y+dy)%4,xhi,core),band))
    def row_y_own(dy):
        return rc(row_src, r_ref.at[wide], r_send.at[dy], r_recv.at[wide], (wid((y+dy)%4,xhi,core),band))
    own_core=rc(row_src, r_ref.at[wide], r_send.at[4], r_recv.at[wide], dev_core)

    def slot(zz,xx,cls): return zz*2+(xx+cls)%2, (xhi+cls)%2
    def unit(b,xs,j): return g2_ref.at[b,xs,pl.ds(j*32,32)]
    def send(src,b,xs,j,sems,dev):
        return rc(src, unit(b,xs,j), sems.at[b,xs,j], g_recv.at[b,xs,j], dev)
    def wait_unit(zz,xx,cls,j):
        b,xs=slot(zz,xx,cls)
        send(unit(b,xs,j),b,xs,j,x_send,dev_x).wait_recv()
        return b,xs
    own_local.wait()
    for q in range(NQ):
        @pl.loop(1,16)
        def _(t):
            a2a_wait(t,q)
        relayout_quarter(rcv,tmp,hold,q)
        @pl.loop(q*2,q*2+2)
        def _(j):
            for cls in range(2):
                b,xs=slot(z,xl,cls)
                src=hold.at[xs,pl.ds(j*32,32)]
                send(src,b,xs,j,x_send,dev_x).start()
                send(src,b,xs,j,zp_send,dev_zp).start()
                send(src,b,xs,j,zm_send,dev_zm).start()
                pltpu.make_async_copy(src,unit(b,xs,j),l_sem.at[2+cls*8+j]).start()
        if q+2<NQ:
            @pl.loop(1,16)
            def _(t):
                a2a_copy(t,q+2).start()
        if q==1:
            rows_xhi.start()
        if q==2:
            for dy in (1,2,3):
                row_y_own(dy).start()
            own_core.start()
    ps=wid(y,1-xhi,core)
    rc(row_src,r_ref.at[ps],r_send.at[0],r_recv.at[ps],dev_x).wait_recv()
    for dy in (1,2,3):
        row_y(dy,ps,4+dy).start()
    rc(r_ref.at[ps],r_ref.at[ps],r_send.at[8],r_recv.at[ps],dev_core).start()
    def pass_core(dy,xh_,slot_):
        s=wid((y+dy)%4,xh_,core)
        rc(row_src,r_ref.at[s],r_send.at[0],r_recv.at[s],dev_x).wait_recv()
        rc(r_ref.at[s],r_ref.at[s],r_send.at[slot_],r_recv.at[s],dev_core).start()
    for dy in (1,3,2):
        pass_core(dy,xhi,8+dy)
    for dy in (1,3,2):
        pass_core(dy,1-xhi,11+dy)
    for dy in range(4):
        for xh_ in range(2):
            s=wid((y+dy)%4,xh_,1-core)
            rc(row_src,r_ref.at[s],r_send.at[0],r_recv.at[s],dev_x).wait_recv()
    row_local.wait()

    def put(b,xs,j,sems,dev):
        send(unit(b,xs,j),b,xs,j,sems,dev).start()

    def near(j):
        b,xs=wait_unit(z,1-xl,0,j)
        put(b,xs,j,zp_send,dev_zp)
        put(b,xs,j,zm_send,dev_zm)
        b2,xs2=wait_unit(zp,xl,1,j)
        @pl.when(j<NA)
        def _():
            put(b2,xs2,j,x_send,dev_x)
        @pl.when(j>=NA)
        def _():
            b1,xs1=wait_unit(z,1-xl,1,j)
            put(b1,xs1,j,zp_send,dev_zp)
            put(b1,xs1,j,zm_send,dev_zm)

    @pl.loop(0,32)
    def _(fg):
        prep_rows(r_ref,fg,rtmp,rt)
        @pl.when(fg%4==3)
        def _():
            near(fg//4)
    rt_copy=pltpu.make_async_copy(rt,rt_out,t_sem)
    rt_copy.start()

    def pass_on(j):
        b,xs=wait_unit(zm,xl,1,j)
        @pl.when(j<NA)
        def _():
            put(b,xs,j,x_send,dev_x)
        @pl.when(j%2==0)
        def _():
            put(b,xs,j,zp_send,dev_zp)
        b3,xs3=slot(zp,xl,1)
        @pl.when(j%2==1)
        def _():
            put(b3,xs3,j,zm_send,dev_zm)

    def pass_own(j):
        b1,xs1=wait_unit(zm,xl,0,j)
        b2,xs2=wait_unit(zp,xl,0,j)
        @pl.when(j%2==0)
        def _():
            put(b1,xs1,j,zp_send,dev_zp)
        @pl.when(j%2==1)
        def _():
            put(b2,xs2,j,zm_send,dev_zm)

    def far(j):
        b,xs=wait_unit(z2,xl,1,j)
        @pl.when(j<NA)
        def _():
            put(b,xs,j,x_send,dev_x)

    def across(zz):
        @pl.loop(0,NA)
        def _(j):
            wait_unit(zz,1-xl,1,j)

    def relay():
        @pl.loop(0,NJ)
        def _(j):
            for zz,parity,sems,dev in ((zm,0,zp_send,dev_zp),(zp,1,zm_send,dev_zm)):
                b,xs=wait_unit(zz,1-xl,0,j)
                @pl.when(j%2==parity)
                def _():
                    put(b,xs,j,sems,dev)
                @pl.when(j>=NA)
                def _():
                    b1,xs1=wait_unit(zz,1-xl,1,j)
                    @pl.when(j%2==parity)
                    def _():
                        put(b1,xs1,j,sems,dev)

    @pl.loop(0,NJ)
    def _(j):
        for cls in range(2):
            b,xs=slot(z,xl,cls)
            pltpu.make_async_copy(hold.at[xs,pl.ds(j*32,32)],unit(b,xs,j),l_sem.at[2+cls*8+j]).wait()
    lag=lag_ref[...]
    @pl.loop(0,3)
    def _(s):
        zz=(z+s+s//2)%4
        @pl.when(s==0)
        def _():
            across(z)
        @pl.when(s==1)
        def _():
            relay()
            across(zp)
        @pl.when(s==2)
        def _():
            across(zm)
        def g_copy(j):
            fs=pl.ds(j*32,32)
            return pltpu.make_async_copy(g2_ref.at[pl.ds(zz*2,2),:,fs],gs.at[:,:,fs],g_sem.at[j])
        for j in range(NJ):
            g_copy(j).start()
        @pl.loop(0,NJ)
        def _(j):
            @pl.when(s==0)
            def _():
                pass_on(j)
            g_copy(j).wait()
            stage_one(gs,rt,scr,j*32,16)
        def o_copy(i):
            return pltpu.make_async_copy(ost.at[i%2],out_ref.at[s,pl.ds(i*16,16)],o_sem.at[i%2])
        @pl.loop(0,8)
        def _(i):
            @pl.when(s==0)
            def _():
                pass_own(i)
            @pl.when(s==1)
            def _():
                far(i)
            @pl.when(i>=2)
            def _():
                o_copy(i).wait()
            stage_two(scr,lag,ost,i%2,i*16,8,band*64,wide*512+zz*128)
            o_copy(i).start()
        o_copy(0).wait()
        o_copy(1).wait()

    @pl.loop(0,NJ)
    def _(j):
        wait_unit(z2,xl,0,j)
        wait_unit(z2,1-xl,0,j)
        wait_unit(z2,1-xl,1,j)
    rt_copy.wait()
    for i in range(15):
        rc(row_src,r_ref.at[wide],r_send.at[i],r_recv.at[wide],dev_x).wait_send()
    @pl.loop(1,16)
    def _(t):
        for q in range(NQ):
            a2a_copy(t,q).wait_send()
    def ws(zz,xx,cls,j,sems):
        b,xs=slot(zz,xx,cls)
        send(unit(b,xs,j),b,xs,j,sems,dev_x).wait_send()
    @pl.loop(0,NJ)
    def _(j):
        for cls in range(2):
            b,xs=slot(z,xl,cls)
            ws(z,xl,cls,j,x_send)
            ws(z,xl,cls,j,zp_send); ws(z,xl,cls,j,zm_send)
        ws(z,1-xl,0,j,zp_send); ws(z,1-xl,0,j,zm_send)
        @pl.when(j>=NA)
        def _():
            ws(z,1-xl,1,j,zp_send); ws(z,1-xl,1,j,zm_send)
        @pl.when(j<NA)
        def _():
            for zz in (zm,zp,z2): ws(zz,xl,1,j,x_send)
        for zz,parity,sems in ((zm,0,zp_send),(zp,1,zm_send)):
            @pl.when(j%2==parity)
            def _():
                ws(zz,xl,0,j,sems); ws(zz,xl,1,j,sems); ws(zz,1-xl,0,j,sems)
                @pl.when(j>=NA)
                def _():
                    ws(zz,1-xl,1,j,sems)


def main(x,lag):
    D=pltpu.SemaphoreType.DMA
    A=pl.BlockSpec(memory_space=pl.ANY)
    bf=jnp.bfloat16
    return pl.pallas_call(main_kernel,
      in_specs=[A,pl.BlockSpec(memory_space=pltpu.VMEM)],
      out_specs=[A]*3,
      out_shape=[jax.ShapeDtypeStruct((3,128,128,128),bf),jax.ShapeDtypeStruct((8,2,256,16,128),bf),jax.ShapeDtypeStruct((128,256,128),bf)],
      scratch_shapes=[pltpu.VMEM((16,2,32,16,128),bf),pltpu.VMEM((2,8,32,16,128),bf),pltpu.VMEM((2,8*PW,128),jnp.float32),pltpu.VMEM((2,256,16,128),bf),
        pltpu.VMEM((2,2,8*PW,128),jnp.float32),pltpu.VMEM((128,256,128),bf),
        pltpu.VMEM((2,2,256,16,128),bf),pltpu.VMEM((256*PITCH,128),jnp.float32),pltpu.VMEM((2,16,128,128),bf),
        D((16,4)),D((16,4)),D((16,)),D((16,)),D((8,2,8)),D((8,2,8)),D((8,2,8)),D((8,2,8)),D((18,)),D((8,)),D((2,)),D(())],
      compiler_params=pltpu.CompilerParams(collective_id=0,has_side_effects=True,vmem_limit_bytes=60*2**20),
    )(x,lag)


def last_kernel(info_ref,lag_ref,rt_ref,g_ref,done_ref,out_ref,scr,ost,buf,c_sem,o_sem):
    t=pl.program_id(0)
    z=info_ref[2]
    far=(z+2)%4
    def take(c):
        return pltpu.make_async_copy(done_ref.at[c//4,pl.ds((c%4)*32,32)],buf.at[c%2],c_sem.at[0,c%2])
    def give(c):
        s=c//4
        return pltpu.make_async_copy(buf.at[c%2],out_ref.at[pl.ds((c%4)*32,32),(z+s+s//2)%4],c_sem.at[1,c%2])
    @pl.when(t==0)
    def _():
        take(0).start()
    take(t).wait()
    @pl.when(t>=1)
    def _():
        give(t-1).wait()
    @pl.when(t<11)
    def _():
        take(t+1).start()
    give(t).start()
    @pl.when(t<4)
    def _():
        @pl.loop(0,2)
        def _(i0):
            for i in range(16):
                parts=[]
                zero=jnp.zeros((64,128),jnp.bfloat16)
                for j in range(2):
                    f=i0*32+2*i+j
                    c=jnp.concatenate(join2(g_ref[0,:,f].reshape(32,128),g_ref[1,:,f].reshape(32,128)),0)
                    parts.append(jnp.concatenate([c,zero] if j==0 else [zero,c],1))
                s=jnp.dot(rt_ref[i0*16+i],jnp.concatenate(parts,0),preferred_element_type=jnp.float32)
                for j in range(2):
                    scr[pl.ds(pl.multiple_of((t*64+i0*32+2*i+j)*PITCH,8),256),:]=s[:,j*128:(j+1)*128]
    @pl.when(t>=4)
    def _():
        i=t-4
        def o_copy(i):
            return pltpu.make_async_copy(ost.at[i%2],out_ref.at[pl.ds(i*16,16),far],o_sem.at[i%2])
        @pl.when(i>=2)
        def _():
            o_copy(i).wait()
        stage_two(scr,lag_ref[...],ost,i%2,i*16,8,info_ref[0],info_ref[1]+far*128)
        o_copy(i).start()
        @pl.when(i==7)
        def _():
            o_copy(0).wait()
            o_copy(1).wait()
            give(11).wait()


def last(info,lag,rt,g2,done):
    D=pltpu.SemaphoreType.DMA
    A=pl.BlockSpec(memory_space=pl.ANY)
    q=lambda t: jnp.minimum(t,3)
    return pl.pallas_call(last_kernel,
      grid_spec=pltpu.PrefetchScalarGridSpec(num_scalar_prefetch=1,grid=(12,),
        in_specs=[pl.BlockSpec((128,512),lambda t,i:(0,0)),
          pl.BlockSpec((32,256,128),lambda t,i:(q(t),0,0)),
          pl.BlockSpec((2,2,64,16,128),lambda t,i:((i[2]+2)%4,0,q(t),0,0)),A],
        out_specs=A,
        scratch_shapes=[pltpu.VMEM((256*PITCH,128),jnp.float32),pltpu.VMEM((2,16,128,128),jnp.bfloat16),pltpu.VMEM((2,32,128,128),jnp.bfloat16),D((2,2)),D((2,))]),
      out_shape=jax.ShapeDtypeStruct((128,4,128,128),jnp.bfloat16),
      compiler_params=pltpu.CompilerParams(vmem_limit_bytes=60*2**20),
    )(info,lag,rt,g2,done)


def body(samples, offsets):
    x = spectra(samples, offsets)
    lag = jnp.asarray(lag_np(), dtype=jnp.bfloat16)
    done, g2, rt = main(x, lag)
    band = lax.axis_index("band")
    info = jnp.stack([band * 64, lax.axis_index("wide") * 512, band // 2]).astype(jnp.int32)
    return last(info, lag, rt, g2, done).reshape(2, 64, 512, 128)


def solution(mesh):
    return jax.shard_map(
        body,
        mesh=mesh,
        in_specs=(P(None, "band", "wide"), P("wide")),
        out_specs=P(None, "band", "wide", None),
        check_vma=False,
    )
```

profile of v0, /device:TPU:1, one launch (start us, length us, event | category | flops | bytes accessed | tf_op | source)
XLA Modules:
  0.0 172.1 jit_solution(9426664851050112738)
XLA Ops:
  0.0 0.6 pad_add_fusion.info_ref
  0.7 0.0 copy-start.1
  0.7 1.7 copy-done.1
  2.3 0.0 copy-start.2
  2.3 1.3 copy-done.2
  3.6 0.0 copy-start.3
  3.6 0.7 copy-done.3
  4.3 6.7 %shard_map.46.x_ref = bf16[16,32,16,128]{3,2,1,0:T(8,128)(2,1)S(1)} custom-call(s32[2]{0:T(128)S(1)} %copy-done.3, f32[512,640]{1,0:T(8,128)S(1)} %copy-done.2, bf16[16,64,1152]{2,1,0:T(8,128)(2,1)S(1)} %copy-done.1), custom_call_target="tpu_custom_call" | custom-call | tf_op jit(solution)/shard_map/pallas_call | solution.py:59
  11.0 0.0 copy-start
  11.0 1.3 copy-done
  12.3 135.5 %shard_map.47 = (bf16[3,128,128,128]{3,2,1,0:T(8,128)(2,1)}, bf16[8,2,256,16,128]{4,3,2,1,0:T(8,128)(2,1)}, bf16[128,256,128]{2,1,0:T(8,128)(2,1)}) custom-call(bf16[16,32,16,128]{3,2,1,0:T(8,128)(2,1)} %copy-done, bf16[128,512]{1,0:T(8,128)(2,1)} %constant.32.clone.lag_ref), custom_call_target="tpu_custom_call" | custom-call | tf_op jit(solution)/shard_map/pallas_call | solution.py:400
  147.8 24.4 %shard_map.48 = bf16[128,4,128,128]{3,2,1,0:T(8,128)(2,1)} custom-call(s32[3]{0:T(128)} %pad_add_fusion.info_ref, bf16[128,512]{1,0:T(8,128)(2,1)} %constant.32.clone.lag_ref, bf16[128,256,128]{2,1,0:T(8,128)(2,1)} %get-tuple-element.8.rt_ref, bf16[8,2,256,16,128]{4,3,2,1,0:T(8,128)(2,1)} %get-tuple-element.9.g_ref, ...), custom_call_target="tpu_custom_call" | custom-call | tf_op jit(solution)/shard_map/pallas_call | solution.py:467
Async XLA Ops:
  0.7 1.7 copy-start.1
  2.3 1.3 copy-start.2
  3.6 0.7 copy-start.3
  11.0 1.3 copy-start
where the time goes:
time: 173 us; the launch traced here: 172 us
  Pallas kernels  167 us (97%)
  local copies, waits for them, and re-layouts  4.95 us (3%)
    pallas_call x1, Pallas kernels, main(): pl.pallas_call(main_kernel, in_specs=[A, pl.BlockSpec(memory_space=pltpu....  135 us
    pallas_call x1, Pallas kernels, last(): pl.pallas_call(last_kernel, grid_spec=pltpu.PrefetchScalarGridSpec(num_sc...  24.4 us
    pallas_call x1, Pallas kernels, spectra(): pl.pallas_call(spec_kernel, grid=(8,), in_specs=[pl.BlockSpec(memory_spac...  6.66 us
    unnamed x8, local copies, waits for them, and re-layouts  4.95 us

commit v1 on v0

--- a/solution.py
+++ b/solution.py
@@ -39,7 +39,7 @@
     @pl.when(i==0)
     def _():
         for k in range(2):
-            t=pltpu.roll(tab_ref[...], off_ref[k]+64*k, 1)
+            t=pltpu.roll(tab_ref[...].astype(jnp.float32), off_ref[k]+64*k, 1)
             tk[k]=t.astype(jnp.bfloat16)
     s=s_ref[...].reshape(128,1152)
     a0=lax.dot_general(tk[0], s[:, :640], (((1,),(1,)),((),())), preferred_element_type=jnp.float32)
@@ -62,8 +62,8 @@
       out_specs=pl.BlockSpec((2,32,16,128),lambda i:(i,0,0,0)),
       out_shape=jax.ShapeDtypeStruct((16,32,16,128),jnp.bfloat16),
       scratch_shapes=[pltpu.VMEM((2,512,640),jnp.bfloat16)],
-      compiler_params=pltpu.CompilerParams(vmem_limit_bytes=32*2**20),
-    )(offsets, jnp.asarray(dft_np()), samples)
+      compiler_params=pltpu.CompilerParams(vmem_limit_bytes=62*2**20),
+    )(offsets, jnp.asarray(dft_np(), dtype=jnp.bfloat16), samples)
 
 def relayout_quarter(rcv, tmp, hold, q):
     @pl.loop(0, 8)
@@ -210,28 +210,9 @@
         if q==1:
             rows_xhi.start()
         if q==2:
-            for dy in (1,2,3):
+            for dy in (1,3):
                 row_y_own(dy).start()
             own_core.start()
-    ps=wid(y,1-xhi,core)
-    rc(row_src,r_ref.at[ps],r_send.at[0],r_recv.at[ps],dev_x).wait_recv()
-    for dy in (1,2,3):
-        row_y(dy,ps,4+dy).start()
-    rc(r_ref.at[ps],r_ref.at[ps],r_send.at[8],r_recv.at[ps],dev_core).start()
-    def pass_core(dy,xh_,slot_):
-        s=wid((y+dy)%4,xh_,core)
-        rc(row_src,r_ref.at[s],r_send.at[0],r_recv.at[s],dev_x).wait_recv()
-        rc(r_ref.at[s],r_ref.at[s],r_send.at[slot_],r_recv.at[s],dev_core).start()
-    for dy in (1,3,2):
-        pass_core(dy,xhi,8+dy)
-    for dy in (1,3,2):
-        pass_core(dy,1-xhi,11+dy)
-    for dy in range(4):
-        for xh_ in range(2):
-            s=wid((y+dy)%4,xh_,1-core)
-            rc(row_src,r_ref.at[s],r_send.at[0],r_recv.at[s],dev_x).wait_recv()
-    row_local.wait()
-
     def put(b,xs,j,sems,dev):
         send(unit(b,xs,j),b,xs,j,sems,dev).start()
 
@@ -249,12 +230,45 @@
             put(b1,xs1,j,zp_send,dev_zp)
             put(b1,xs1,j,zm_send,dev_zm)
 
+    def row_wait(s):
+        rc(row_src,r_ref.at[s],r_send.at[0],r_recv.at[s],dev_x).wait_recv()
+
+    def pass_core(dy,xh_,slot_):
+        s=wid((y+dy)%4,xh_,core)
+        row_wait(s)
+        rc(r_ref.at[s],r_ref.at[s],r_send.at[slot_],r_recv.at[s],dev_core).start()
+        return s
+
+    near(0)
+    ps=wid(y,1-xhi,core)
+    row_wait(ps)
+    row_y(1,ps,5).start()
+    row_y(3,ps,7).start()
+    rc(r_ref.at[ps],r_ref.at[ps],r_send.at[8],r_recv.at[ps],dev_core).start()
+    near(1)
+    near(2)
+    s3=pass_core(3,xhi,10)
+    row_y(1,s3,2).start()
+    pass_core(1,xhi,9)
+    near(3)
+    s1=pass_core(1,1-xhi,12)
+    row_y(3,s1,6).start()
+    pass_core(3,1-xhi,13)
+    near(4)
+    pass_core(2,xhi,11)
+    near(5)
+    pass_core(2,1-xhi,14)
+    for dy in range(4):
+        for xh_ in range(2):
+            row_wait(wid((y+dy)%4,xh_,1-core))
+    row_local.wait()
+
     @pl.loop(0,32)
     def _(fg):
         prep_rows(r_ref,fg,rtmp,rt)
-        @pl.when(fg%4==3)
-        def _():
-            near(fg//4)
+        @pl.when(fg%16==7)
+        def _():
+            near(6+fg//16)
     rt_copy=pltpu.make_async_copy(rt,rt_out,t_sem)
     rt_copy.start()
 
@@ -413,22 +427,27 @@
     t=pl.program_id(0)
     z=info_ref[2]
     far=(z+2)%4
-    def take(c):
-        return pltpu.make_async_copy(done_ref.at[c//4,pl.ds((c%4)*32,32)],buf.at[c%2],c_sem.at[0,c%2])
-    def give(c):
+    def takes(c):
+        return [pltpu.make_async_copy(done_ref.at[c//4,pl.ds((c%4)*32+8*h,8)],buf.at[c%3,pl.ds(8*h,8)],c_sem.at[0,c%3,h]) for h in range(4)]
+    def gives(c):
         s=c//4
-        return pltpu.make_async_copy(buf.at[c%2],out_ref.at[pl.ds((c%4)*32,32),(z+s+s//2)%4],c_sem.at[1,c%2])
+        return [pltpu.make_async_copy(buf.at[c%3,pl.ds(8*h,8)],out_ref.at[pl.ds((c%4)*32+8*h,8),(z+s+s//2)%4],c_sem.at[1,c%3,h]) for h in range(4)]
     @pl.when(t==0)
     def _():
-        take(0).start()
-    take(t).wait()
+        for d in takes(0)+takes(1):
+            d.start()
+    for d in takes(t):
+        d.wait()
+    for d in gives(t):
+        d.start()
     @pl.when(t>=1)
     def _():
-        give(t-1).wait()
-    @pl.when(t<11)
+        for d in gives(t-1):
+            d.wait()
+    @pl.when(t<10)
     def _():
-        take(t+1).start()
-    give(t).start()
+        for d in takes(t+2):
+            d.start()
     @pl.when(t<4)
     def _():
         @pl.loop(0,2)
@@ -457,7 +476,8 @@
         def _():
             o_copy(0).wait()
             o_copy(1).wait()
-            give(11).wait()
+            for d in gives(11):
+                d.wait()
 
 
 def last(info,lag,rt,g2,done):
@@ -470,7 +490,7 @@
           pl.BlockSpec((32,256,128),lambda t,i:(q(t),0,0)),
           pl.BlockSpec((2,2,64,16,128),lambda t,i:((i[2]+2)%4,0,q(t),0,0)),A],
         out_specs=A,
-        scratch_shapes=[pltpu.VMEM((256*PITCH,128),jnp.float32),pltpu.VMEM((2,16,128,128),jnp.bfloat16),pltpu.VMEM((2,32,128,128),jnp.bfloat16),D((2,2)),D((2,))]),
+        scratch_shapes=[pltpu.VMEM((256*PITCH,128),jnp.float32),pltpu.VMEM((2,16,128,128),jnp.bfloat16),pltpu.VMEM((3,32,128,128),jnp.bfloat16),D((2,3,4)),D((2,))]),
       out_shape=jax.ShapeDtypeStruct((128,4,128,128),jnp.bfloat16),
       compiler_params=pltpu.CompilerParams(vmem_limit_bytes=60*2**20),
     )(info,lag,rt,g2,done)

time: 173 us -> 166 us (0.960)
  local copies, waits for them, and re-layouts: 4.95 us -> 0 us
  Pallas kernels: 167 us -> 165 us
    unnamed x8 -> x0, local copies, waits for them, and re-layouts: 4.95 us -> none
    pallas_call x1, Pallas kernels: 24.4 us -> 20.6 us  [last(): pl.pallas_call(last_kernel, grid_spec=pltpu.PrefetchScalarGridSpec(num_sc...]
    pallas_call x1, Pallas kernels: 6.66 us -> 9.26 us  [spectra(): pl.pallas_call(spec_kernel, grid=(8,), in_specs=[pl.BlockSpec(memory_spac...]
where the time goes in v1:
time: 166 us
  Pallas kernels  165 us (99%)
    pallas_call x1, Pallas kernels, main(): pl.pallas_call(main_kernel, in_specs=[A, pl.BlockSpec(memory_space=pltpu....  136 us
    pallas_call x1, Pallas kernels, last(): pl.pallas_call(last_kernel, grid_spec=pltpu.PrefetchScalarGridSpec(num_sc...  20.6 us
    pallas_call x1, Pallas kernels, spectra(): pl.pallas_call(spec_kernel, grid=(8,), in_specs=[pl.BlockSpec(memory_spac...  9.26 us

profile of v1, /device:TPU:1, one launch (start us, length us, event | category | flops | bytes accessed | tf_op | source)
XLA Modules:
  0.0 166.0 jit_solution(17053071582431063328)
XLA Ops:
  0.0 0.6 pad_add_fusion.info_ref
  0.6 9.3 %shard_map.46.x_ref = bf16[16,32,16,128]{3,2,1,0:T(8,128)(2,1)} custom-call(s32[2]{0:T(128)} %off_ref.1, bf16[512,640]{1,0:T(8,128)(2,1)} %constant.31.clone.tab_ref, bf16[16,64,1152]{2,1,0:T(8,128)(2,1)} %s_ref.1), custom_call_target="tpu_custom_call" | custom-call | tf_op jit(solution)/shard_map/pallas_call | solution.py:59
  9.8 135.6 %shard_map.47 = (bf16[3,128,128,128]{3,2,1,0:T(8,128)(2,1)}, bf16[8,2,256,16,128]{4,3,2,1,0:T(8,128)(2,1)}, bf16[128,256,128]{2,1,0:T(8,128)(2,1)}) custom-call(bf16[16,32,16,128]{3,2,1,0:T(8,128)(2,1)} %shard_map.46.x_ref, bf16[128,512]{1,0:T(8,128)(2,1)} %constant.32.clone.lag_ref), custom_call_target="tpu_custom_call" | custom-call | tf_op jit(solution)/shard_map/pallas_call | solution.py:414
  145.4 20.6 %shard_map.48 = bf16[128,4,128,128]{3,2,1,0:T(8,128)(2,1)} custom-call(s32[3]{0:T(128)} %pad_add_fusion.info_ref, bf16[128,512]{1,0:T(8,128)(2,1)} %constant.32.clone.lag_ref, bf16[128,256,128]{2,1,0:T(8,128)(2,1)} %get-tuple-element.8.rt_ref, bf16[8,2,256,16,128]{4,3,2,1,0:T(8,128)(2,1)} %get-tuple-element.9.g_ref, ...), custom_call_target="tpu_custom_call" | custom-call | tf_op jit(solution)/shard_map/pallas_call | solution.py:487
